TPU v7x, 512 devices: a whole 4x4x16 slice. The times are simulated.
512 devices in a mesh: depth: 4 (over x), row: 8 (over z_lo), col: 16 (over y, z_hi, core).
Axes of the slice: x: 4, y: 4, z: 16 (z_hi: 2, z_lo: 8; z = z_hi * 8 + z_lo), core: 2. Of those that a mesh axis runs over, the one named last changes fastest.
Arguments:
- inputs: bfloat16 [1024, 16384], P('row', 'col'), may hold values from -6 to 6
- out_grad: bfloat16 [1024, 32768], P('col', ('depth', 'row')), may hold values from -6 to 6
- weight: bfloat16 [16384, 32768], P('col', ('depth', 'row')), may hold values from -0.046875 to 0.046875
Outputs:
- input_grad: bfloat16 [1024, 16384], P(('depth', 'row'), 'col')
- weight_grad: bfloat16 [16384, 32768], P('col', ('depth', 'row'))
All inputs are finite; a program needn't handle non-finite values.
Results may differ from a plain program's by a relative error of at most 0.0011.
Values may be sent and summed in bfloat16 or wider, within the bound.
A program may use at most 64 MiB of HBM per device.

v0:
```python
import jax
import jax.numpy as jnp
from jax import lax
from jax.sharding import PartitionSpec as P


def per_device(inputs, out_grad, weight):
    grads_all = lax.all_gather(out_grad, "col", axis=0, tiled=True)
    total_rows = grads_all.shape[0]
    scale = 1.0 / total_rows
    summed = lax.psum_scatter(
        lax.dot_general(
            grads_all, weight, (((1,), (1,)), ((), ())), preferred_element_type=jnp.float32
        ),
        ("depth", "row"),
        scatter_dimension=0,
        tiled=True,
    )
    input_grad = summed.astype(jnp.bfloat16)
    gathered = lax.all_gather(inputs, "row", axis=0, tiled=True)
    product = lax.dot_general(
        gathered, grads_all, (((0,), (0,)), ((), ())), preferred_element_type=jnp.float32
    )
    weight_grad = (product * scale).astype(jnp.bfloat16)
    return (input_grad, weight_grad)


def solution(mesh):
    return jax.shard_map(
        per_device,
        mesh=mesh,
        in_specs=(P("row", "col"), P("col", ("depth", "row")), P("col", ("depth", "row"))),
        out_specs=(P(("depth", "row"), "col"), P("col", ("depth", "row"))),
        check_vma=False,
    )
```

profile of v0, /device:TPU:16, one launch (start us, length us, event | category | flops | bytes accessed | tf_op | source)
XLA Modules:
  0.0 433.3 jit_solution(9945350856612399759)
XLA Ops:
  7.2 0.0 copy-start
  7.2 0.0 all-gather.3.cloned.1.call-start
  7.2 0.7 all-gather.3.cloned.1.call-update
  7.9 0.0 all-gather.5.cloned.1.call-start
  8.0 0.7 all-gather.5.cloned.1.call-update
  8.7 0.0 reduce-scatter.2.cloned.1.call-start
  8.7 97.5 %all-gather.3.cloned.1.call-done = bf16[1024,1024]{1,0:T(8,128)(2,1)} async-done(((bf16[64,1024]{1,0:T(8,128)(2,1)}), bf16[1024,1024]{1,0:T(8,128)(2,1)}) %all-gather.3.cloned.1.call-update) | async-done | bytes 2097168 | tf_op jit(solution)/shard_map/all_gather | solution.py:8
  106.3 0.0 copy-done
  106.3 5.9 %fusion = f32[1024,1024]{1,0:T(8,128)} fusion(bf16[1024,1024]{1,0:T(8,128)(2,1)} %all-gather.3.cloned.1.call-done, bf16[1024,1024]{1,0:T(8,128)(2,1)S(1)} %copy-done), kind=kOutput, calls=%fused_computation.1 | convolution fusion | flops 2147483648 | bytes 8388608 | tf_op jit(solution)/shard_map/dot_general | solution.py:12
  112.2 0.0 reduce-scatter.2.cloned.1.call-update
  112.2 59.5 %all-gather.5.cloned.1.call-done = bf16[1024,1024]{1,0:T(8,128)(2,1)} async-done(((bf16[128,1024]{1,0:T(8,128)(2,1)}), bf16[1024,1024]{1,0:T(8,128)(2,1)}) %all-gather.5.cloned.1.call-update) | async-done | bytes 2097168 | tf_op jit(solution)/shard_map/all_gather | solution.py:20
  171.7 5.9 %multiply_convert_fusion = bf16[1024,1024]{1,0:T(8,128)(2,1)} fusion(bf16[1024,1024]{1,0:T(8,128)(2,1)} %all-gather.5.cloned.1.call-done, bf16[1024,1024]{1,0:T(8,128)(2,1)} %all-gather.3.cloned.1.call-done), kind=kOutput, calls=%fused_computation | convolution fusion | flops 2149580800 | bytes 6291456 | tf_op jit(solution)/shard_map/dot_general | solution.py:21
  177.6 247.6 %reduce-scatter.2.cloned.1.call-done = f32[32,1024]{1,0:T(8,128)} async-done(((f32[1024,1024]{1,0:T(8,128)}), f32[32,1024]{1,0:T(8,128)}) %reduce-scatter.2.cloned.1.call-update) | async-done | bytes 131088 | tf_op jit(solution)/shard_map/reduce_scatter | solution.py:11
  425.2 1.5 convert_element_type.6
Async XLA Ops:
  7.2 99.1 %copy-start = (bf16[1024,1024]{1,0:T(8,128)(2,1)S(1)}, bf16[1024,1024]{1,0:T(8,128)(2,1)}, u32[]{:S(2)}) copy-start(bf16[1024,1024]{1,0:T(8,128)(2,1)} %param.5) | copy-start | bytes 6291460
  7.2 99.1 %all-gather.3.cloned.1.call-start = ((), (), s32[]{:S(2)}) async-start(), calls=%async_computation.1 | async-start | bytes 2228224 | tf_op jit(solution)/shard_map/all_gather | solution.py:8
  7.9 163.8 %all-gather.5.cloned.1.call-start = ((), (), s32[]{:S(2)}) async-start(), calls=%async_computation.3 | async-start | bytes 2359296 | tf_op jit(solution)/shard_map/all_gather | solution.py:20
  8.7 416.6 %reduce-scatter.2.cloned.1.call-start = ((), (), s32[]{:S(2)}) async-start(), calls=%async_computation.2 | async-start | bytes 4325376 | tf_op jit(solution)/shard_map/reduce_scatter | solution.py:11
Sparse Core Ops, SparseCore 0:
  11.3 94.9 all-gather.2
  108.3 63.3 all-gather.4
  174.5 250.6 reduce-scatter.1
where the time goes:
time: 433 us
  waiting for transfers between devices  406 us (94%)
  between operations  13.8 us (3%)
  matrix products  11.8 us (3%)
    reduce_scatter x1, waiting for transfers between devices, per_device(): lax.psum_scatter(lax.dot_general(grads_all, weight, (((1,), (1,)), ((), (...  248 us
    all_gather x1, waiting for transfers between devices, per_device(): grads_all = lax.all_gather(out_grad, 'col', axis=0, tiled=True)  97.5 us
    all_gather x1, waiting for transfers between devices, per_device(): gathered = lax.all_gather(inputs, 'row', axis=0, tiled=True)  59.5 us
  transfers between devices with their start and end apart: 3, of which 3 were waited for; matrix products, arithmetic and copies ran while one was open for 3% of the time, Pallas kernels for 0%

commit v1 on v0

v1 whole, which is shorter than its diff:
```python
import jax
import jax.numpy as jnp
from jax import lax
from jax.experimental import pallas as pl
from jax.experimental.pallas import tpu as pltpu
from jax.sharding import PartitionSpec as P

MESH = pl.DeviceIdType.MESH
F32 = jnp.float32
BF16 = jnp.bfloat16
PEAK = 200.0


def encode(value, code_ref, scale_ref):
    size = jnp.abs(value)
    top = jnp.max(jnp.max(size, axis=0, keepdims=True), axis=1, keepdims=True)
    top = jnp.maximum(top, 1e-30)
    power = size * (PEAK / top)
    for _ in range(4):
        power = power * power
    code_ref[...] = jnp.where(value < 0, -power, power).astype(BF16)
    scale_ref[...] = jnp.broadcast_to(top * (1.0 / PEAK), scale_ref.shape)


def decode(code_ref, scale_ref):
    code = code_ref[...].astype(F32)
    size = jnp.exp2(jnp.log2(jnp.abs(code)) * 0.0625)
    size = jnp.where(code == 0, 0.0, size) * scale_ref[0:1, 0:1]
    return jnp.where(code < 0, -size, size)


def kernel(
    x_hbm, g_hbm, w_hbm, ig_ref, dw_hbm,
    w, g, xs, acc, dw, part, own, fin,
    xc_s, xc_r, xk_s, xk_r,
    zc_s, zc_r, zk_s, zk_r,
    bc_s, bc_r, bk_s, bk_r,
    local, out_sem,
    gz_s, gz_r, gy_s, gy_r, gk_s, gk_r,
    cx_s, cx_r, kx_s, kx_r,
    cz_s, cz_r, kz_s, kz_r,
    cb_s, cb_r,
    xz_s, xz_r, xx_s, xx_r,
):
    x = lax.axis_index("depth")
    zl = lax.axis_index("row")
    col = lax.axis_index("col")
    y, zh, core = col // 4, (col // 2) % 2, col % 2
    quad, pos = zl // 4, zl % 4

    def y_dev(o):
        return (x, zl, lax.rem(y + o, 4) * 4 + zh * 2 + core)

    def x_dev(o):
        return (lax.rem(x + o, 4), zl, col)

    def q_dev(o):
        return (x, quad * 4 + lax.rem(pos + o, 4), col)

    z8_dev = (x, zl, y * 4 + (1 - zh) * 2 + core)
    sib_dev = (x, zl, y * 4 + zh * 2 + (1 - core))
    z4_dev = (x, (1 - quad) * 4 + pos, col)

    def remote(src, dst, send, recv, device):
        return pltpu.make_async_remote_copy(
            src_ref=src, dst_ref=dst, send_sem=send, recv_sem=recv, device_id=device, device_id_type=MESH
        )

    def g_rows(yy, zz, kk):
        return pl.ds(pl.multiple_of(yy * 256 + zz * 128 + kk * 64, 64), 64)

    load_w = pltpu.make_async_copy(w_hbm, w, local.at[0])
    load_g = pltpu.make_async_copy(g_hbm, g.at[g_rows(y, zh, core)], local.at[1])
    load_w.start()
    load_g.start()
    loads_x = []
    for q in range(4):
        c = pltpu.make_async_copy(x_hbm.at[pl.ds(q * 32, 32)], xs.at[zl, q], local.at[2 + q])
        c.start()
        loads_x.append(c)

    barrier = pltpu.get_barrier_semaphore()
    partners = [z8_dev, sib_dev, z4_dev]
    partners += [f(o) for f in (y_dev, x_dev, q_dev) for o in (1, 2, 3)]
    for device in partners:
        pl.semaphore_signal(barrier, inc=1, device_id=device, device_id_type=MESH)
    pl.semaphore_wait(barrier, len(partners))

    pending = []

    gz = remote(g_hbm, g.at[g_rows(y, zh, core)], gz_s, gz_r, z8_dev)
    gz.start()
    pending.append(gz)

    def spread(ph, zz, src):
        for o in (1, 3, 2):
            c = remote(src, g.at[g_rows(y, zz, core)], gy_s.at[ph, o - 1], gy_r.at[ph, o - 1], y_dev(o))
            c.start()
            pending.append(c)
        c = remote(src, g.at[g_rows(y, zz, core)], gk_s.at[ph, 0], gk_r.at[ph, 0], sib_dev)
        c.start()
        pending.append(c)

    def forward(ph, zz, o):
        rows = g_rows(lax.rem(y + 4 - o, 4), zz, core)
        remote(g.at[rows], g.at[rows], gy_s.at[ph, o - 1], gy_r.at[ph, o - 1], y_dev(o)).wait_recv()
        c = remote(g.at[rows], g.at[rows], gk_s.at[ph, o], gk_r.at[ph, o], sib_dev)
        c.start()
        pending.append(c)

    def from_sibling(ph, zz, o):
        rows = g_rows(lax.rem(y + 4 - o, 4), zz, 1 - core)
        remote(g.at[rows], g.at[rows], gk_s.at[ph, o], gk_r.at[ph, o], sib_dev).wait_recv()

    def partial(ph, zz, o):
        target = lax.rem(y + 4 - o, 4)
        rows = pl.ds(pl.multiple_of(target * 256 + zz * 128, 128), 128)

        @pl.loop(0, 4)
        def _(t):
            cols = pl.ds(pl.multiple_of(t * 256, 256), 256)
            part[:, cols] = lax.dot_general(
                g[rows, :], w[cols, :], (((1,), (1,)), ((), ())), preferred_element_type=F32
            )

        @pl.when(target == x)
        def _():
            own[ph] = part[...]

        @pl.when(target != x)
        def _():
            slot = lax.rem(x - target + 4, 4) - 1
            encode(part[...], xc_s.at[ph, slot], xk_s.at[ph, slot])
            device = (target, zl, col)
            remote(xc_s.at[ph, slot], xc_r.at[ph, slot], cx_s.at[ph, slot], cx_r.at[ph, slot], device).start()
            remote(xk_s.at[ph, slot], xk_r.at[ph, slot], kx_s.at[ph, slot], kx_r.at[ph, slot], device).start()

    def sum_x(ph):
        for s in range(3):
            remote(xc_s.at[ph, s], xc_r.at[ph, s], cx_s.at[ph, s], cx_r.at[ph, s], x_dev(1)).wait_recv()
            remote(xk_s.at[ph, s], xk_r.at[ph, s], kx_s.at[ph, s], kx_r.at[ph, s], x_dev(1)).wait_recv()

        @pl.loop(0, 4)
        def _(b):
            rows = pl.ds(pl.multiple_of(b * 32, 32), 32)
            total = own[ph, rows, :]
            for s in range(3):
                total = total + decode(xc_r.at[ph, s, rows], xk_r.at[ph, s])
            own[ph, rows, :] = total

        for o in (1, 2, 3):
            rows = pl.ds(pl.multiple_of(lax.rem(pos + o, 4) * 32, 32), 32)
            s = o - 1
            encode(own[ph, rows, :], zc_s.at[ph, s], zk_s.at[ph, s])
            c = remote(zc_s.at[ph, s], zc_r.at[ph, s], cz_s.at[ph, s], cz_r.at[ph, s], q_dev(o))
            c.start()
            pending.append(c)
            c = remote(zk_s.at[ph, s], zk_r.at[ph, s], kz_s.at[ph, s], kz_r.at[ph, s], q_dev(o))
            c.start()
            pending.append(c)

    def cross(i):
        code = remote(bc_s, bc_r, cb_s.at[0], cb_r.at[0], z4_dev)
        scale = remote(bk_s, bk_r, cb_s.at[1], cb_r.at[1], z4_dev)
        return code, scale

    def sum_quad(ph, zz):
        total = own[ph, pl.ds(pl.multiple_of(pos * 32, 32), 32), :]
        for s in range(3):
            remote(zc_s.at[ph, s], zc_r.at[ph, s], cz_s.at[ph, s], cz_r.at[ph, s], q_dev(1)).wait_recv()
            remote(zk_s.at[ph, s], zk_r.at[ph, s], kz_s.at[ph, s], kz_r.at[ph, s], q_dev(1)).wait_recv()
            total = total + decode(zc_r.at[ph, s], zk_r.at[ph, s])
        fin[ph] = total

        @pl.when(zz != quad)
        def _():
            encode(fin[ph], bc_s, bk_s)
            for c in cross(0):
                c.start()

    spread(0, zh, g_hbm)
    load_g.wait()
    load_w.wait()
    from_sibling(0, zh, 0)
    partial(0, zh, 0)
    forward(0, zh, 1)
    forward(0, zh, 3)
    from_sibling(0, zh, 1)
    partial(0, zh, 1)
    from_sibling(0, zh, 3)
    partial(0, zh, 3)
    forward(0, zh, 2)
    from_sibling(0, zh, 2)
    partial(0, zh, 2)

    far = 1 - zh
    far_rows = g_rows(y, far, core)
    remote(g.at[far_rows], g.at[far_rows], gz_s, gz_r, z8_dev).wait_recv()
    spread(1, far, g.at[far_rows])

    mine = x_hbm.at[pl.ds(pl.multiple_of(x * 32, 32), 32)]
    for o in (1, 2, 3):
        c = remote(mine, xs.at[zl, x], xz_s.at[o - 1], xz_r.at[o - 1], q_dev(o))
        c.start()
        pending.append(c)
    c = remote(mine, xs.at[zl, x], xz_s.at[3], xz_r.at[3], z4_dev)
    c.start()
    pending.append(c)

    from_sibling(1, far, 0)
    partial(1, far, 0)
    forward(1, far, 1)
    forward(1, far, 3)
    from_sibling(1, far, 1)
    partial(1, far, 1)
    from_sibling(1, far, 3)
    partial(1, far, 3)
    forward(1, far, 2)
    from_sibling(1, far, 2)
    partial(1, far, 2)

    sum_x(0)

    zo = (1 - quad) * 4 + pos
    remote(xs.at[zo, x], xs.at[zo, x], xz_s.at[3], xz_r.at[3], z4_dev).wait_recv()
    for o in (1, 2, 3):
        c = remote(xs.at[zo, x], xs.at[zo, x], xz_s.at[3 + o], xz_r.at[3 + o], q_dev(o))
        c.start()
        pending.append(c)

    sum_quad(0, zh)
    sum_x(1)

    for o in (1, 2, 3):
        zs = quad * 4 + lax.rem(pos + 4 - o, 4)
        remote(xs.at[zs, x], xs.at[zs, x], xz_s.at[o - 1], xz_r.at[o - 1], q_dev(1)).wait_recv()
        for p in (1, 3, 2):
            c = remote(xs.at[zs, x], xs.at[zs, x], xx_s.at[p - 1, o - 1], xx_r.at[p - 1, o - 1], x_dev(p))
            c.start()
            pending.append(c)
    for o in (1, 2, 3):
        zs = (1 - quad) * 4 + lax.rem(pos + 4 - o, 4)
        remote(xs.at[zs, x], xs.at[zs, x], xz_s.at[3 + o], xz_r.at[3 + o], q_dev(1)).wait_recv()
    others = pl.ds(pl.multiple_of((1 - quad) * 4, 4), 4)
    for p in (1, 3, 2):
        c = remote(xs.at[others, x], xs.at[others, x], xx_s.at[p - 1, 3], xx_r.at[p - 1, 3], x_dev(p))
        c.start()
        pending.append(c)

    sum_quad(1, far)

    for c in loads_x:
        c.wait()
    for p in (1, 2, 3):
        xo = lax.rem(x + 4 - p, 4)
        for o in (1, 2, 3):
            zs = quad * 4 + lax.rem(pos + 4 - o, 4)
            remote(xs.at[zs, xo], xs.at[zs, xo], xx_s.at[p - 1, o - 1], xx_r.at[p - 1, o - 1], x_dev(p)).wait_recv()

    def product(qd, t):
        rows = pl.ds(pl.multiple_of(qd * 4, 4), 4)
        cols = pl.ds(pl.multiple_of(t * 256, 256), 256)
        lhs = xs[rows, :, :, cols].reshape(512, 256)
        rhs = g[pl.ds(pl.multiple_of(qd * 512, 512), 512), :]
        return lax.dot_general(lhs, rhs, (((0,), (0,)), ((), ())), preferred_element_type=F32)

    @pl.loop(0, 4)
    def _(t):
        acc[pl.ds(pl.multiple_of(t * 256, 256), 256), :] = product(quad, t)

    for c in cross(0):
        c.wait_recv()
    mine_ph = jnp.where(quad == zh, 0, 1)
    ig_ref[...] = (fin[mine_ph] + decode(bc_r, bk_r)).astype(BF16)

    for p in (1, 2, 3):
        xo = lax.rem(x + 4 - p, 4)
        remote(xs.at[others, xo], xs.at[others, xo], xx_s.at[p - 1, 3], xx_r.at[p - 1, 3], x_dev(p)).wait_recv()

    @pl.loop(0, 4)
    def _(t):
        rows = pl.ds(pl.multiple_of(t * 256, 256), 256)
        dw[rows, :] = ((acc[rows, :] + product(1 - quad, t)) * (1.0 / 1024)).astype(BF16)
        pltpu.make_async_copy(dw.at[rows], dw_hbm.at[rows], out_sem.at[t]).start()

    for c in pending:
        c.wait_send()
    for c in cross(0):
        c.wait_send()
    for ph in range(2):
        for s in range(3):
            remote(xc_s.at[ph, s], xc_r.at[ph, s], cx_s.at[ph, s], cx_r.at[ph, s], x_dev(1)).wait_send()
            remote(xk_s.at[ph, s], xk_r.at[ph, s], kx_s.at[ph, s], kx_r.at[ph, s], x_dev(1)).wait_send()

    @pl.loop(0, 4)
    def _(t):
        rows = pl.ds(pl.multiple_of(t * 256, 256), 256)
        pltpu.make_async_copy(dw.at[rows], dw_hbm.at[rows], out_sem.at[t]).wait()


def per_device(inputs, out_grad, weight):
    dma = pltpu.SemaphoreType.DMA
    vmem = pltpu.VMEM
    return pl.pallas_call(
        kernel,
        out_shape=(
            jax.ShapeDtypeStruct((32, 1024), BF16),
            jax.ShapeDtypeStruct((1024, 1024), BF16),
        ),
        in_specs=[pl.BlockSpec(memory_space=pl.ANY)] * 3,
        out_specs=(pl.BlockSpec(memory_space=vmem), pl.BlockSpec(memory_space=pl.ANY)),
        scratch_shapes=[
            vmem((1024, 1024), BF16),
            vmem((1024, 1024), BF16),
            vmem((8, 4, 32, 1024), BF16),
            vmem((1024, 1024), F32),
            vmem((1024, 1024), BF16),
            vmem((128, 1024), F32),
            vmem((2, 128, 1024), F32),
            vmem((2, 32, 1024), F32),
            vmem((2, 3, 128, 1024), BF16),
            vmem((2, 3, 128, 1024), BF16),
            vmem((2, 3, 8, 128), F32),
            vmem((2, 3, 8, 128), F32),
            vmem((2, 3, 32, 1024), BF16),
            vmem((2, 3, 32, 1024), BF16),
            vmem((2, 3, 8, 128), F32),
            vmem((2, 3, 8, 128), F32),
            vmem((32, 1024), BF16),
            vmem((32, 1024), BF16),
            vmem((8, 128), F32),
            vmem((8, 128), F32),
            dma((6,)),
            dma((4,)),
            dma,
            dma,
            dma((2, 3)),
            dma((2, 3)),
            dma((2, 4)),
            dma((2, 4)),
            dma((2, 3)),
            dma((2, 3)),
            dma((2, 3)),
            dma((2, 3)),
            dma((2, 3)),
            dma((2, 3)),
            dma((2, 3)),
            dma((2, 3)),
            dma((2,)),
            dma((2,)),
            dma((7,)),
            dma((7,)),
            dma((3, 4)),
            dma((3, 4)),
        ],
        compiler_params=pltpu.CompilerParams(
            collective_id=0, has_side_effects=True, vmem_limit_bytes=48 * 1024 * 1024
        ),
        cost_estimate=pl.CostEstimate(flops=4 * 1024**3, bytes_accessed=7 * 1024**2, transcendentals=0),
        name="grads",
    )(inputs, out_grad, weight)


def solution(mesh):
    return jax.shard_map(
        per_device,
        mesh=mesh,
        in_specs=(P("row", "col"), P("col", ("depth", "row")), P("col", ("depth", "row"))),
        out_specs=(P(("depth", "row"), "col"), P("col", ("depth", "row"))),
        check_vma=False,
    )
```

time: 433 us -> 89.4 us (0.21)
  the two profiles are of different devices: /device:TPU:16 before, /device:TPU:40 now
where the time goes in v1:
time: 89.4 us; the launch traced here: 89.2 us
  Pallas kernels  83.2 us (93%)
  local copies, waits for them, and re-layouts  5.39 us (6%)
    pallas_call x1, Pallas kernels, per_device(): pl.pallas_call(kernel, out_shape=(jax.ShapeDtypeStruct((32, 1024), BF16),...  83.2 us
    unnamed x8, local copies, waits for them, and re-layouts  5.39 us

profile of v1, /device:TPU:40, one launch (start us, length us, event | category | flops | bytes accessed | tf_op | source)
XLA Modules:
  0.0 89.2 jit_solution(18392980085705712527)
XLA Ops:
  0.6 0.0 copy-start
  0.6 1.6 %copy-done = bf16[1024,1024]{1,0:T(8,128)(2,1)S(1)} copy-done((bf16[1024,1024]{1,0:T(8,128)(2,1)S(1)}, bf16[1024,1024]{1,0:T(8,128)(2,1)}, u32[]{:S(2)}) %copy-start) | copy-done | bytes 2097176
  2.2 0.0 copy-start.1
  2.2 0.9 %copy-done.1 = bf16[128,1024]{1,0:T(8,128)(2,1)S(1)} copy-done((bf16[128,1024]{1,0:T(8,128)(2,1)S(1)}, bf16[128,1024]{1,0:T(8,128)(2,1)}, u32[]{:S(2)}) %copy-start.1) | copy-done | bytes 262168
  3.2 0.0 copy-start.2
  3.2 0.9 %copy-done.2 = bf16[64,1024]{1,0:T(8,128)(2,1)S(1)} copy-done((bf16[64,1024]{1,0:T(8,128)(2,1)S(1)}, bf16[64,1024]{1,0:T(8,128)(2,1)}, u32[]{:S(2)}) %copy-start.2) | copy-done | bytes 131096
  4.1 83.2 %grads.1 = (bf16[32,1024]{1,0:T(8,128)(2,1)S(1)}, bf16[1024,1024]{1,0:T(8,128)(2,1)S(1)}) custom-call(bf16[128,1024]{1,0:T(8,128)(2,1)S(1)} %copy-done.1, bf16[64,1024]{1,0:T(8,128)(2,1)S(1)} %copy-done.2, bf16[1024,1024]{1,0:T(8,128)(2,1)S(1)} %copy-done), custom_call_target="tpu_custom_call" | custom-call | flops 4294967296 | bytes 7340032 | tf_op jit(solution)/shard_map/grads/pallas_call | solution.py:304
  87.3 0.6 copy.7
  87.9 1.3 %copy.8 = bf16[1024,1024]{1,0:T(8,128)(2,1)} copy(bf16[1024,1024]{1,0:T(8,128)(2,1)S(1)} %get-tuple-element.5) | data formatting | bytes 4194304
Async XLA Ops:
  0.6 1.6 %copy-start = (bf16[1024,1024]{1,0:T(8,128)(2,1)S(1)}, bf16[1024,1024]{1,0:T(8,128)(2,1)}, u32[]{:S(2)}) copy-start(bf16[1024,1024]{1,0:T(8,128)(2,1)} %w_hbm.1) | copy-start | bytes 6291460
  2.2 0.9 %copy-start.1 = (bf16[128,1024]{1,0:T(8,128)(2,1)S(1)}, bf16[128,1024]{1,0:T(8,128)(2,1)}, u32[]{:S(2)}) copy-start(bf16[128,1024]{1,0:T(8,128)(2,1)} %x_hbm.1) | copy-start | bytes 786436
  3.2 0.9 %copy-start.2 = (bf16[64,1024]{1,0:T(8,128)(2,1)S(1)}, bf16[64,1024]{1,0:T(8,128)(2,1)}, u32[]{:S(2)}) copy-start(bf16[64,1024]{1,0:T(8,128)(2,1)} %g_hbm.1) | copy-start | bytes 393220

commit v2 on v0

v2 whole, which is shorter than its diff:
```python
import jax
import jax.numpy as jnp
from jax import lax
from jax.experimental import pallas as pl
from jax.experimental.pallas import tpu as pltpu
from jax.sharding import PartitionSpec as P

MESH = pl.DeviceIdType.MESH
F32 = jnp.float32
BF16 = jnp.bfloat16
PEAK = 200.0


def encode(value, code_ref, scale_ref):
    size = jnp.abs(value)
    top = jnp.max(jnp.max(size, axis=0, keepdims=True), axis=1, keepdims=True)
    top = jnp.maximum(top, 1e-30)
    power = size * (PEAK / top)
    for _ in range(4):
        power = power * power
    code_ref[...] = jnp.where(value < 0, -power, power).astype(BF16)
    scale_ref[...] = jnp.broadcast_to(top * (1.0 / PEAK), scale_ref.shape)


def decode(code_ref, scale_ref):
    code = code_ref[...].astype(F32)
    size = jnp.exp2(jnp.log2(jnp.abs(code)) * 0.0625)
    size = jnp.where(code == 0, 0.0, size) * scale_ref[0:1, 0:1]
    return jnp.where(code < 0, -size, size)


def kernel(
    x_hbm, g_hbm, w_hbm, ig_ref, dw_hbm,
    w, g, xs, acc, dw, part, own, fin,
    xc_s, xc_r, xk_s, xk_r,
    zc_s, zc_r, zk_s, zk_r,
    bc_s, bc_r, bk_s, bk_r,
    local, out_sem, near_in, far_in,
    gz_s, gz_r, gy_s, gy_r, gk_s, gk_r,
    cx_s, cx_r, kx_s, kx_r,
    cz_s, cz_r, kz_s, kz_r,
    cb_s, cb_r,
    xz_s, xz_r, xx_s, xx_r,
):
    x = lax.axis_index("depth")
    zl = lax.axis_index("row")
    col = lax.axis_index("col")
    y, zh, core = col // 4, (col // 2) % 2, col % 2
    quad, pos = zl // 4, zl % 4

    def y_dev(o):
        return (x, zl, lax.rem(y + o, 4) * 4 + zh * 2 + core)

    def x_dev(o):
        return (lax.rem(x + o, 4), zl, col)

    def q_dev(o):
        return (x, quad * 4 + lax.rem(pos + o, 4), col)

    z8_dev = (x, zl, y * 4 + (1 - zh) * 2 + core)
    sib_dev = (x, zl, y * 4 + zh * 2 + (1 - core))
    z4_dev = (x, (1 - quad) * 4 + pos, col)

    def remote(src, dst, send, recv, device):
        return pltpu.make_async_remote_copy(
            src_ref=src, dst_ref=dst, send_sem=send, recv_sem=recv, device_id=device, device_id_type=MESH
        )

    load_w = pltpu.make_async_copy(w_hbm, w, local.at[0])
    load_g = pltpu.make_async_copy(g_hbm, g.at[y, zh, core], local.at[1])
    load_w.start()
    load_g.start()
    loads_x = []
    for q in range(4):
        c = pltpu.make_async_copy(x_hbm.at[pl.ds(q * 32, 32)], xs.at[zl, q], local.at[2 + q])
        c.start()
        loads_x.append(c)

    def signal(semaphore, device):
        pl.semaphore_signal(semaphore, inc=1, device_id=device, device_id_type=MESH)

    barrier = pltpu.get_barrier_semaphore()
    for device in [sib_dev] + [f(o) for f in (y_dev, x_dev) for o in (1, 2, 3)]:
        signal(barrier, device)
    for o in (1, 2, 3):
        pl.when(pos + o < 4)(lambda o=o: signal(barrier, q_dev(o)))
    pl.when(quad == 0)(lambda: signal(barrier, z4_dev))
    pl.when(zh == 0)(lambda: signal(barrier, z8_dev))
    pl.semaphore_wait(barrier, 7 + pos + quad + zh)
    pl.when(zh == 1)(lambda: signal(far_in, z8_dev))
    for o in (1, 2, 3):
        pl.when(pos + o >= 4)(lambda o=o: signal(near_in, q_dev(o)))
    pl.when(quad == 1)(lambda: signal(near_in, z4_dev))

    pending = []

    far = 1 - zh
    to_far = [remote(g_hbm.at[pl.ds(32 * h, 32)], g.at[y, zh, core, pl.ds(32 * h, 32)], gz_s.at[h], gz_r.at[h], z8_dev) for h in (0, 1)]
    pending += to_far

    @pl.when(zh == 1)
    def _():
        for c in to_far:
            c.start()

    def chunk(yy, zz, kk, h):
        return g.at[yy, zz, kk, pl.ds(32 * h, 32)]

    def spread(ph, h, zz):
        src = chunk(y, zz, core, h)
        for o in (1, 3, 2):
            c = remote(src, src, gy_s.at[ph, h, o - 1], gy_r.at[ph, h, o - 1], y_dev(o))
            c.start()
            pending.append(c)
        c = remote(src, src, gk_s.at[ph, h, 0], gk_r.at[ph, h, 0], sib_dev)
        c.start()
        pending.append(c)

    def collect(ph, h, zz):
        for o in (1, 3, 2):
            block = chunk(lax.rem(y + 4 - o, 4), zz, core, h)
            remote(block, block, gy_s.at[ph, h, o - 1], gy_r.at[ph, h, o - 1], y_dev(o)).wait_recv()
            c = remote(block, block, gk_s.at[ph, h, o], gk_r.at[ph, h, o], sib_dev)
            c.start()
            pending.append(c)
        for o in (0, 1, 3, 2):
            block = chunk(lax.rem(y + 4 - o, 4), zz, 1 - core, h)
            remote(block, block, gk_s.at[ph, h, o], gk_r.at[ph, h, o], sib_dev).wait_recv()

    def partial(ph, h, zz):
        part[...] = lax.dot_general(
            g[:, zz, :, pl.ds(32 * h, 32), :].reshape(256, 1024),
            w[...],
            (((1,), (1,)), ((), ())),
            preferred_element_type=F32,
        )

        for o in (2, 1, 3):
            target = lax.rem(x + o, 4)
            rows = pl.ds(pl.multiple_of(target * 64, 64), 64)
            s = o - 1
            encode(part[rows, :], xc_s.at[ph, h, s], xk_s.at[ph, h, s])
            c = remote(xc_s.at[ph, h, s], xc_r.at[ph, h, s], cx_s.at[ph, h, s], cx_r.at[ph, h, s], x_dev(o))
            c.start()
            pending.append(c)
            c = remote(xk_s.at[ph, h, s], xk_r.at[ph, h, s], kx_s.at[ph, h, s], kx_r.at[ph, h, s], x_dev(o))
            c.start()
            pending.append(c)
        own[ph, h] = part[pl.ds(pl.multiple_of(x * 64, 64), 64), :]

    def to_quad(ph, slot, device):
        code = remote(zc_s.at[ph, slot], zc_r.at[ph, slot], cz_s.at[ph, slot], cz_r.at[ph, slot], device)
        scale = remote(zk_s.at[ph, slot], zk_r.at[ph, slot], kz_s.at[ph, slot], kz_r.at[ph, slot], device)
        return code, scale

    def sum_x(ph, h):
        for s in range(3):
            remote(xc_s.at[ph, h, s], xc_r.at[ph, h, s], cx_s.at[ph, h, s], cx_r.at[ph, h, s], x_dev(1)).wait_recv()
            remote(xk_s.at[ph, h, s], xk_r.at[ph, h, s], kx_s.at[ph, h, s], kx_r.at[ph, h, s], x_dev(1)).wait_recv()
        for k in (0, 1):
            rows = pl.ds(k * 32, 32)
            total = own[ph, h, rows, :]
            for s in range(3):
                total = total + decode(xc_r.at[ph, h, s, rows], xk_r.at[ph, h, s])
            own[ph, h, rows, :] = total
            there = 2 * k + h

            @pl.when(pos != there)
            def _():
                slot = lax.rem(there - pos + 4, 4) - 1
                encode(own[ph, h, rows, :], zc_s.at[ph, slot], zk_s.at[ph, slot])
                for c in to_quad(ph, slot, (x, quad * 4 + there, col)):
                    c.start()

    def cross():
        code = remote(bc_s, bc_r, cb_s.at[0], cb_r.at[0], z4_dev)
        scale = remote(bk_s, bk_r, cb_s.at[1], cb_r.at[1], z4_dev)
        return code, scale

    def sum_quad(ph, h, zz):
        @pl.when(lax.rem(pos, 2) == h)
        def _():
            total = own[ph, h, pl.ds(pl.multiple_of(pos // 2 * 32, 32), 32), :]
            for s in range(3):
                for c in to_quad(ph, s, q_dev(1)):
                    c.wait_recv()
                total = total + decode(zc_r.at[ph, s], zk_r.at[ph, s])
            fin[ph] = total

            @pl.when(zz != quad)
            def _():
                encode(fin[ph], bc_s, bk_s)
                for c in cross():
                    c.start()

    def near_spread():
        load_g.wait()
        for h in (0, 1):
            spread(0, h, zh)
        load_w.wait()

    def near_part(h):
        collect(0, h, zh)
        partial(0, h, zh)

    def far_send():
        @pl.when(zh == 0)
        def _():
            pl.semaphore_wait(far_in, 1)
            for c in to_far:
                c.start()

    def far_take(h):
        block = chunk(y, far, core, h)
        remote(block, block, gz_s.at[h], gz_r.at[h], z8_dev).wait_recv()
        spread(1, h, far)

    def far_part(h):
        collect(1, h, far)
        partial(1, h, far)

    mine = x_hbm.at[pl.ds(pl.multiple_of(x * 32, 32), 32)]
    zo = (1 - quad) * 4 + pos
    others = pl.ds(pl.multiple_of((1 - quad) * 4, 4), 4)

    def rows_z(piece, i, device):
        return remote(piece, piece, xz_s.at[i], xz_r.at[i], device)

    def x_quad():
        @pl.when(pos + quad < 4)
        def _():
            pl.semaphore_wait(near_in, (3 - pos) + (1 - quad))

        for o in (1, 2, 3):
            c = remote(mine, xs.at[zl, x], xz_s.at[o - 1], xz_r.at[o - 1], q_dev(o))
            c.start()
            pending.append(c)

    def x_other():
        c = remote(mine, xs.at[zl, x], xz_s.at[3], xz_r.at[3], z4_dev)
        c.start()
        pending.append(c)

    def x_pass():
        rows_z(xs.at[zo, x], 3, z4_dev).wait_recv()
        for o in (1, 2, 3):
            c = rows_z(xs.at[zo, x], 3 + o, q_dev(o))
            c.start()
            pending.append(c)

    def rows_x(hop, way, i, q, lines):
        if i < 3:
            piece = xs.at[quad * 4 + lax.rem(pos + 3 - i, 4), lax.rem(q, 4), lines]
        else:
            piece = xs.at[others, lax.rem(q, 4), lines]
        return remote(piece, piece, xx_s.at[hop, way, i], xx_r.at[hop, way, i], x_dev(3 if way else 1))

    ALL, HALF = pl.ds(0, 32), (pl.ds(0, 16), pl.ds(16, 16))

    def x_row(i):
        if i < 3:
            rows_z(xs.at[quad * 4 + lax.rem(pos + 3 - i, 4), x], i, q_dev(1)).wait_recv()
        else:
            for o in (1, 2, 3):
                rows_z(xs.at[(1 - quad) * 4 + lax.rem(pos + 4 - o, 4), x], 3 + o, q_dev(1)).wait_recv()
        for way in (0, 1):
            c = rows_x(0, way, i, x, ALL)
            c.start()
            pending.append(c)

    def x_row_pass(i):
        for way in (0, 1):
            q = x + 1 if way else x + 3
            rows_x(0, way, i, q, ALL).wait_recv()
            c = rows_x(1, way, i, q, HALF[way])
            c.start()
            pending.append(c)

    def x_row_end(i):
        for way in (0, 1):
            rows_x(1, way, i, x + 2, HALF[way]).wait_recv()

    def x_row_quad():
        for i in range(3):
            x_row(i)

    def x_row_quad_pass():
        for i in range(3):
            x_row_pass(i)

    def product(qd, t):
        rows = pl.ds(pl.multiple_of(qd * 4, 4), 4)
        cols = pl.ds(pl.multiple_of(t * 256, 256), 256)
        lhs = xs[rows, :, :, cols].reshape(512, 256)
        rhs = g[pl.ds(pl.multiple_of(qd * 2, 2), 2)].reshape(512, 1024)
        return lax.dot_general(lhs, rhs, (((0,), (0,)), ((), ())), preferred_element_type=F32)

    def weight_quad():
        for c in loads_x:
            c.wait()
        for i in range(3):
            x_row_end(i)

        @pl.loop(0, 4)
        def _(t):
            acc[pl.ds(pl.multiple_of(t * 256, 256), 256), :] = product(quad, t)

    def weight_other():
        x_row_end(3)

        @pl.loop(0, 4)
        def _(t):
            rows = pl.ds(pl.multiple_of(t * 256, 256), 256)
            dw[rows, :] = ((acc[rows, :] + product(1 - quad, t)) * (1.0 / 1024)).astype(BF16)
            pltpu.make_async_copy(dw.at[rows], dw_hbm.at[rows], out_sem.at[t]).start()

    def input_grad():
        for c in cross():
            c.wait_recv()
        mine_ph = jnp.where(quad == zh, 0, 1)
        ig_ref[...] = (fin[mine_ph] + decode(bc_r, bk_r)).astype(BF16)

    near_spread()
    near_part(0)
    far_send()
    near_part(1)
    far_take(0)
    far_take(1)
    x_quad()
    x_other()
    sum_x(0, 0)
    sum_x(0, 1)
    far_part(0)
    far_part(1)
    x_pass()
    sum_quad(0, 0, zh)
    sum_quad(0, 1, zh)
    x_row_quad()
    sum_x(1, 0)
    x_row_quad_pass()
    sum_x(1, 1)
    x_row(3)
    sum_quad(1, 0, far)
    sum_quad(1, 1, far)
    x_row_pass(3)
    weight_quad()
    input_grad()
    weight_other()

    for c in pending:
        c.wait_send()
    for c in cross():
        c.wait_send()
    for ph in (0, 1):
        for s in range(3):
            for c in to_quad(ph, s, q_dev(1)):
                c.wait_send()

    @pl.loop(0, 4)
    def _(t):
        rows = pl.ds(pl.multiple_of(t * 256, 256), 256)
        pltpu.make_async_copy(dw.at[rows], dw_hbm.at[rows], out_sem.at[t]).wait()


def per_device(inputs, out_grad, weight):
    dma = pltpu.SemaphoreType.DMA
    vmem = pltpu.VMEM
    return pl.pallas_call(
        kernel,
        out_shape=(
            jax.ShapeDtypeStruct((32, 1024), BF16),
            jax.ShapeDtypeStruct((1024, 1024), BF16),
        ),
        in_specs=[pl.BlockSpec(memory_space=pl.ANY)] * 3,
        out_specs=(pl.BlockSpec(memory_space=vmem), pl.BlockSpec(memory_space=pl.ANY)),
        scratch_shapes=[
            vmem((1024, 1024), BF16),
            vmem((4, 2, 2, 64, 1024), BF16),
            vmem((8, 4, 32, 1024), BF16),
            vmem((1024, 1024), F32),
            vmem((1024, 1024), BF16),
            vmem((256, 1024), F32),
            vmem((2, 2, 64, 1024), F32),
            vmem((2, 32, 1024), F32),
            vmem((2, 2, 3, 64, 1024), BF16),
            vmem((2, 2, 3, 64, 1024), BF16),
            vmem((2, 2, 3, 8, 128), F32),
            vmem((2, 2, 3, 8, 128), F32),
            vmem((2, 3, 32, 1024), BF16),
            vmem((2, 3, 32, 1024), BF16),
            vmem((2, 3, 8, 128), F32),
            vmem((2, 3, 8, 128), F32),
            vmem((32, 1024), BF16),
            vmem((32, 1024), BF16),
            vmem((8, 128), F32),
            vmem((8, 128), F32),
            dma((6,)),
            dma((4,)),
            pltpu.SemaphoreType.REGULAR,
            pltpu.SemaphoreType.REGULAR,
            dma((2,)),
            dma((2,)),
            dma((2, 2, 3)),
            dma((2, 2, 3)),
            dma((2, 2, 4)),
            dma((2, 2, 4)),
            dma((2, 2, 3)),
            dma((2, 2, 3)),
            dma((2, 2, 3)),
            dma((2, 2, 3)),
            dma((2, 3)),
            dma((2, 3)),
            dma((2, 3)),
            dma((2, 3)),
            dma((2,)),
            dma((2,)),
            dma((7,)),
            dma((7,)),
            dma((2, 2, 4)),
            dma((2, 2, 4)),
        ],
        compiler_params=pltpu.CompilerParams(
            collective_id=0, has_side_effects=True, vmem_limit_bytes=63 * 1024 * 1024
        ),
        cost_estimate=pl.CostEstimate(flops=4 * 1024**3, bytes_accessed=7 * 1024**2, transcendentals=0),
        name="grads",
    )(inputs, out_grad, weight)


def solution(mesh):
    return jax.shard_map(
        per_device,
        mesh=mesh,
        in_specs=(P("row", "col"), P("col", ("depth", "row")), P("col", ("depth", "row"))),
        out_specs=(P(("depth", "row"), "col"), P("col", ("depth", "row"))),
        check_vma=False,
    )
```

time: 433 us -> 78.7 us (0.18)
  the two profiles are of different devices: /device:TPU:16 before, /device:TPU:448 now
where the time goes in v2:
time: 78.7 us; the launch traced here: 78.5 us
  Pallas kernels  73.3 us (93%)
  local copies, waits for them, and re-layouts  4.55 us (6%)
    pallas_call x1, Pallas kernels, per_device(): pl.pallas_call(kernel, out_shape=(jax.ShapeDtypeStruct((32, 1024), BF16),...  73.3 us
    unnamed x2, local copies, waits for them, and re-layouts  4.55 us

profile of v2, /device:TPU:448, one launch (start us, length us, event | category | flops | bytes accessed | tf_op | source)
XLA Modules:
  0.0 78.5 jit_solution(15143665295346495458)
XLA Ops:
  0.6 73.3 %grads.1 = (bf16[32,1024]{1,0:T(8,128)(2,1)}, bf16[1024,1024]{1,0:T(8,128)(2,1)}) custom-call(bf16[128,1024]{1,0:T(8,128)(2,1)} %x_hbm.1, bf16[64,1024]{1,0:T(8,128)(2,1)} %g_hbm.1, bf16[1024,1024]{1,0:T(8,128)(2,1)} %w_hbm.1), custom_call_target="tpu_custom_call" | custom-call | flops 4294967296 | bytes 7340032 | tf_op jit(solution)/shard_map/grads/pallas_call | solution.py:368
  74.0 1.5 %copy.7 = bf16[32,1024]{1,0:T(8,128)(2,1)} copy(bf16[32,1024]{1,0:T(8,128)(2,1)} %get-tuple-element.4) | data formatting | bytes 131072
  75.4 3.1 %copy.8 = bf16[1024,1024]{1,0:T(8,128)(2,1)} copy(bf16[1024,1024]{1,0:T(8,128)(2,1)} %get-tuple-element.5) | data formatting | bytes 4194304

commit v3 on v2

--- a/solution.py
+++ b/solution.py
@@ -107,12 +107,13 @@
         return g.at[yy, zz, kk, pl.ds(32 * h, 32)]
 
     def spread(ph, h, zz):
-        src = chunk(y, zz, core, h)
+        src = g_hbm.at[pl.ds(32 * h, 32)] if ph == 0 else chunk(y, zz, core, h)
+        dst = chunk(y, zz, core, h)
         for o in (1, 3, 2):
-            c = remote(src, src, gy_s.at[ph, h, o - 1], gy_r.at[ph, h, o - 1], y_dev(o))
-            c.start()
-            pending.append(c)
-        c = remote(src, src, gk_s.at[ph, h, 0], gk_r.at[ph, h, 0], sib_dev)
+            c = remote(src, dst, gy_s.at[ph, h, o - 1], gy_r.at[ph, h, o - 1], y_dev(o))
+            c.start()
+            pending.append(c)
+        c = remote(src, dst, gk_s.at[ph, h, 0], gk_r.at[ph, h, 0], sib_dev)
         c.start()
         pending.append(c)
 
@@ -194,9 +195,9 @@
                     c.start()
 
     def near_spread():
-        load_g.wait()
         for h in (0, 1):
             spread(0, h, zh)
+        load_g.wait()
         load_w.wait()
 
     def near_part(h):
@@ -321,23 +322,23 @@
         ig_ref[...] = (fin[mine_ph] + decode(bc_r, bk_r)).astype(BF16)
 
     near_spread()
+    x_quad()
     near_part(0)
     far_send()
     near_part(1)
     far_take(0)
     far_take(1)
-    x_quad()
     x_other()
+    x_row_quad()
     sum_x(0, 0)
     sum_x(0, 1)
     far_part(0)
     far_part(1)
     x_pass()
+    x_row_quad_pass()
     sum_quad(0, 0, zh)
     sum_quad(0, 1, zh)
-    x_row_quad()
     sum_x(1, 0)
-    x_row_quad_pass()
     sum_x(1, 1)
     x_row(3)
     sum_quad(1, 0, far)

time: 78.7 us -> 74.9 us (0.952)
  Pallas kernels: 73.3 us -> 69.5 us
    pallas_call x1, Pallas kernels: 73.3 us -> 69.5 us  [per_device(): pl.pallas_call(kernel, out_shape=(jax.ShapeDtypeStruct((32, 1024), BF16),...]
where the time goes in v3:
time: 74.9 us; the launch traced here: 74.7 us
  Pallas kernels  69.5 us (93%)
  local copies, waits for them, and re-layouts  4.55 us (6%)
    pallas_call x1, Pallas kernels, per_device(): pl.pallas_call(kernel, out_shape=(jax.ShapeDtypeStruct((32, 1024), BF16),...  69.5 us
    unnamed x2, local copies, waits for them, and re-layouts  4.55 us

profile of v3, /device:TPU:448, one launch (start us, length us, event | category | flops | bytes accessed | tf_op | source)
XLA Modules:
  0.0 74.7 jit_solution(2712812978776716902)
XLA Ops:
  0.6 69.5 %grads.1 = (bf16[32,1024]{1,0:T(8,128)(2,1)}, bf16[1024,1024]{1,0:T(8,128)(2,1)}) custom-call(bf16[128,1024]{1,0:T(8,128)(2,1)} %x_hbm.1, bf16[64,1024]{1,0:T(8,128)(2,1)} %g_hbm.1, bf16[1024,1024]{1,0:T(8,128)(2,1)} %w_hbm.1), custom_call_target="tpu_custom_call" | custom-call | flops 4294967296 | bytes 7340032 | tf_op jit(solution)/shard_map/grads/pallas_call | solution.py:369
  70.2 1.5 %copy.7 = bf16[32,1024]{1,0:T(8,128)(2,1)} copy(bf16[32,1024]{1,0:T(8,128)(2,1)} %get-tuple-element.4) | data formatting | bytes 131072
  71.6 3.1 %copy.8 = bf16[1024,1024]{1,0:T(8,128)(2,1)} copy(bf16[1024,1024]{1,0:T(8,128)(2,1)} %get-tuple-element.5) | data formatting | bytes 4194304

commit v4 on v3

--- a/solution.py
+++ b/solution.py
@@ -95,7 +95,10 @@
     pending = []
 
     far = 1 - zh
-    to_far = [remote(g_hbm.at[pl.ds(32 * h, 32)], g.at[y, zh, core, pl.ds(32 * h, 32)], gz_s.at[h], gz_r.at[h], z8_dev) for h in (0, 1)]
+    to_far = []
+    for i in range(4):
+        lines = pl.ds(16 * i, 16)
+        to_far.append(remote(g_hbm.at[lines], g.at[y, zh, core, lines], gz_s.at[i], gz_r.at[i], z8_dev))
     pending += to_far
 
     @pl.when(zh == 1)
@@ -109,7 +112,7 @@
     def spread(ph, h, zz):
         src = g_hbm.at[pl.ds(32 * h, 32)] if ph == 0 else chunk(y, zz, core, h)
         dst = chunk(y, zz, core, h)
-        for o in (1, 3, 2):
+        for o in (2, 1, 3):
             c = remote(src, dst, gy_s.at[ph, h, o - 1], gy_r.at[ph, h, o - 1], y_dev(o))
             c.start()
             pending.append(c)
@@ -212,8 +215,9 @@
                 c.start()
 
     def far_take(h):
-        block = chunk(y, far, core, h)
-        remote(block, block, gz_s.at[h], gz_r.at[h], z8_dev).wait_recv()
+        for i in (2 * h, 2 * h + 1):
+            block = g.at[y, far, core, pl.ds(16 * i, 16)]
+            remote(block, block, gz_s.at[i], gz_r.at[i], z8_dev).wait_recv()
         spread(1, h, far)
 
     def far_part(h):
@@ -330,9 +334,9 @@
     far_take(1)
     x_other()
     x_row_quad()
+    far_part(0)
     sum_x(0, 0)
     sum_x(0, 1)
-    far_part(0)
     far_part(1)
     x_pass()
     x_row_quad_pass()
@@ -341,10 +345,10 @@
     sum_x(1, 0)
     sum_x(1, 1)
     x_row(3)
+    weight_quad()
     sum_quad(1, 0, far)
     sum_quad(1, 1, far)
     x_row_pass(3)
-    weight_quad()
     input_grad()
     weight_other()
 
@@ -399,8 +403,8 @@
             dma((4,)),
             pltpu.SemaphoreType.REGULAR,
             pltpu.SemaphoreType.REGULAR,
-            dma((2,)),
-            dma((2,)),
+            dma((4,)),
+            dma((4,)),
             dma((2, 2, 3)),
             dma((2, 2, 3)),
             dma((2, 2, 4)),

time: 74.9 us -> 74.6 us (level)
  the two profiles are of different devices: /device:TPU:448 before, /device:TPU:34 now
where the time goes in v4:
time: 74.6 us; the launch traced here: 74.4 us
  Pallas kernels  69.2 us (93%)
  local copies, waits for them, and re-layouts  4.55 us (6%)
    pallas_call x1, Pallas kernels, per_device(): pl.pallas_call(kernel, out_shape=(jax.ShapeDtypeStruct((32, 1024), BF16),...  69.2 us
    unnamed x2, local copies, waits for them, and re-layouts  4.55 us

profile of v4, /device:TPU:34, one launch (start us, length us, event | category | flops | bytes accessed | tf_op | source)
XLA Modules:
  0.0 74.4 jit_solution(321586466343073489)
XLA Ops:
  0.6 69.2 %grads.1 = (bf16[32,1024]{1,0:T(8,128)(2,1)}, bf16[1024,1024]{1,0:T(8,128)(2,1)}) custom-call(bf16[128,1024]{1,0:T(8,128)(2,1)} %x_hbm.1, bf16[64,1024]{1,0:T(8,128)(2,1)} %g_hbm.1, bf16[1024,1024]{1,0:T(8,128)(2,1)} %w_hbm.1), custom_call_target="tpu_custom_call" | custom-call | flops 4294967296 | bytes 7340032 | tf_op jit(solution)/shard_map/grads/pallas_call | solution.py:373
  69.8 1.5 %copy.7 = bf16[32,1024]{1,0:T(8,128)(2,1)} copy(bf16[32,1024]{1,0:T(8,128)(2,1)} %get-tuple-element.4) | data formatting | bytes 131072
  71.3 3.1 %copy.8 = bf16[1024,1024]{1,0:T(8,128)(2,1)} copy(bf16[1024,1024]{1,0:T(8,128)(2,1)} %get-tuple-element.5) | data formatting | bytes 4194304
